TPU v7x, 32 devices: a whole 2x2x4 slice. The times are simulated.
32 devices in a mesh: member: 8 (over z, core), state: 4 (over y, x).
Axes of the slice: x: 2, y: 2, z: 4, core: 2. Of those that a mesh axis runs over, the one named last changes fastest.
Arguments:
- prior_analyses: float32 [64, 256, 1024], P('member', 'state'), may hold values from -6 to 6
- smoothing_number: float32 [256, 1024], P('state'), may hold values from 0.08 to 0.24
- observations: float32 [3072], replicated, may hold values from -6 to 6
- obs_variance: float32 [3072], replicated, may hold values from 0.25 to 2
- obs_row: int32 [3072], replicated, may hold values from 0 to 255
- obs_col: int32 [3072], replicated, may hold values from 0 to 1023
- obs_radius: int32 [3072], replicated, may hold values from 32 to 127
- block_order: int32 [3072], replicated, may hold values from 0 to 3071, each once
Outputs:
- analysis: float32 [64, 256, 1024], P('member', 'state')
Inputs may be any that keep to these rules, and one draw needn't show every extreme that they name: `block_order`: every observation index appears exactly once.
All inputs are finite; a program needn't handle non-finite values.
Results may differ from a plain program's by a relative error of at most 0.0035.
Values sent between devices are 32-bit elements; how exact they have to be, the bound alone decides.
A program may use at most 64 MiB of HBM per device.

v0:
```python
import jax
import jax.numpy as jnp
from jax import lax
from jax.sharding import PartitionSpec as P

BLK = 512
NBLK = 6
spread_eps = 1e-06


def extended(shard, sides, width):
    for axis, dim in sides:
        peers, length = (lax.axis_size(axis), shard.shape[dim])
        up = [(i, (i + 1) % peers) for i in range(peers - 1)]
        down = [(j, i) for i, j in up]
        last = lax.slice_in_dim(shard, length - width, length, axis=dim)
        leading = lax.slice_in_dim(shard, 0, width, axis=dim)
        before = lax.ppermute(last, axis, up)
        after = lax.ppermute(leading, axis, down)
        shard = jnp.concatenate([before, shard, after], axis=dim)
    return shard


def advance(padded, spreading_coefficients):
    center = padded[:, 1:-1, :]
    vertical = padded[:, 2:, :] + padded[:, :-2, :]
    sideways = jnp.pad(center[:, :, 1:], ((0, 0), (0, 0), (0, 1))) + jnp.pad(
        center[:, :, :-1], ((0, 0), (0, 0), (1, 0))
    )
    return center + spreading_coefficients * (vertical + sideways - 4.0 * center)


def predicted_level(realization_vectors, spreading_coefficients):
    current = realization_vectors
    for step_index in range(2):
        padded = extended(current, (("state", 1),), 1)
        current = advance(padded, spreading_coefficients)
    return current


def increments(prior_values, value_array, variances):
    realization_vectors = prior_values.shape[0]
    prior_mean = jnp.mean(prior_values, axis=0)
    anomaly = prior_values - prior_mean
    spread = jnp.sum(anomaly * anomaly, axis=0) / (realization_vectors - 1) + spread_eps
    post_var = spread * variances / (spread + variances)
    posterior_average = post_var * (prior_mean / spread + value_array / variances)
    shrink = jnp.sqrt(variances / (variances + spread)) - 1.0
    increment = (posterior_average - prior_mean + shrink * anomaly).astype(jnp.bfloat16)
    return (anomaly.astype(jnp.bfloat16), increment, 1.0 / spread)


def taper_weight(cell_row, cell_col, obs_rows, obs_cols, radius):
    row_gap = cell_row[None, :] - obs_rows[:, None]
    col_gap = cell_col[None, :] - obs_cols[:, None]
    distance = (row_gap * row_gap + col_gap * col_gap).astype(jnp.float32)
    reach = radius.astype(jnp.float32)
    closeness = jnp.maximum(1.0 - distance / (reach * reach)[:, None], 0.0)
    return closeness * closeness


def linear_gain_fit(
    target, target_rows, target_cols, anomaly, increment, inverse, obs_rows, obs_cols, radius
):
    realization_vectors = target.shape[0]
    cell_mean = jnp.mean(target, axis=0)
    cell_anomaly = (target - cell_mean).astype(jnp.bfloat16)
    sub_size = min(anomaly.shape[1], 128)
    accumulated = jnp.zeros(target.shape, jnp.float32)
    for part_index in range(anomaly.shape[1] // sub_size):
        lower_end = part_index * sub_size
        upper_end = lower_end + sub_size
        covariance = lax.dot_general(
            anomaly[:, lower_end:upper_end],
            cell_anomaly,
            (((0,), (0,)), ((), ())),
            preferred_element_type=jnp.float32,
        ) / (realization_vectors - 1)
        weight = taper_weight(
            target_rows,
            target_cols,
            obs_rows[lower_end:upper_end],
            obs_cols[lower_end:upper_end],
            radius[lower_end:upper_end],
        )
        gain_tile = (weight * covariance * inverse[lower_end:upper_end, None]).astype(jnp.bfloat16)
        accumulated = accumulated + jnp.dot(
            increment[:, lower_end:upper_end], gain_tile, preferred_element_type=jnp.float32
        )
    return accumulated


def pick_values(cell_values, rows_wanted, cols_wanted, first_row, tile_rows, tile_cols):
    local_row = rows_wanted - first_row
    inside = (
        (local_row >= 0) & (local_row < tile_rows) & (cols_wanted >= 0) & (cols_wanted < tile_cols)
    )
    local_index = jnp.where(inside, local_row * tile_cols + cols_wanted, 0)
    return jnp.where(inside[None, :], jnp.take(cell_values, local_index, axis=1), 0.0)


def on_device(
    prior_analyses,
    smoothing_number,
    observations,
    obs_variance,
    obs_row,
    obs_col,
    obs_radius,
    block_order,
):
    realization_vectors = predicted_level(prior_analyses, smoothing_number)
    row_count = realization_vectors.shape[1]
    col_count = realization_vectors.shape[2]
    member_count = lax.axis_size("member")
    base_row = lax.axis_index("state") * row_count
    tile_data = lax.all_to_all(
        realization_vectors, "member", split_axis=1, concat_axis=0, tiled=True
    )
    tile_rows = row_count // member_count
    first_row = base_row + lax.axis_index("member") * tile_rows
    grid_point_total = tile_rows * col_count
    cell_values = tile_data.reshape(tile_data.shape[0], grid_point_total)
    position = jnp.arange(grid_point_total, dtype=jnp.int32)
    cell_row = first_row + position // col_count
    cell_col = position % col_count
    for block_index in range(NBLK):
        chosen = block_order[block_index * BLK : (block_index + 1) * BLK]
        block_rows = jnp.take(obs_row, chosen)
        block_cols = jnp.take(obs_col, chosen)
        block_radius = jnp.take(obs_radius, chosen)
        local_values = pick_values(
            cell_values, block_rows, block_cols, first_row, tile_rows, col_count
        )
        prior_values = lax.psum(local_values, ("member", "state"))
        anomaly, increment, inverse = increments(
            prior_values, jnp.take(observations, chosen), jnp.take(obs_variance, chosen)
        )
        cell_values = cell_values + linear_gain_fit(
            cell_values,
            cell_row,
            cell_col,
            anomaly,
            increment,
            inverse,
            block_rows,
            block_cols,
            block_radius,
        )
    result = cell_values.reshape(tile_data.shape)
    return lax.all_to_all(result, "member", split_axis=0, concat_axis=1, tiled=True)


def solution(mesh):
    in_specs = (P("member", "state", None), P("state", None), P(), P(), P(), P(), P(), P())
    out_specs = P("member", "state", None)
    return jax.shard_map(
        on_device, mesh=mesh, in_specs=in_specs, out_specs=out_specs, check_vma=False
    )
```

profile of v0, /device:TPU:0, one launch (start us, length us, event | category | flops | bytes accessed | tf_op | source)
XLA Modules:
  0.0 1187.5 jit_solution(11396176168441743626)
XLA Ops:
  140.1 45.9 %all-to-all-done = f32[8,64,1024]{2,0,1:T(8,128)S(1)} async-done(((f32[8,64,1024]{2,0,1:T(8,128)}), f32[8,64,1024]{2,0,1:T(8,128)S(1)}, u32[]{:S(2)}, u32[]{:S(2)}) %all-to-all-start) | async-done | bytes 2097184 | tf_op jit(solution)/shard_map/all_to_all | solution.py:117
  193.2 124.2 %all-reduce.11.cloned.1.call-done = f32[64,512]{0,1:T(8,128)} async-done(((f32[64,512]{0,1:T(8,128)}), f32[64,512]{0,1:T(8,128)}) %all-reduce.11.cloned.1.call-update) | async-done | bytes 131088 | tf_op jit(solution)/shard_map/psum | solution.py:135
  330.4 5.6 convolution_add_fusion.16
  336.0 5.7 fusion.292
  350.1 123.9 %all-reduce.13.cloned.1.call-done = f32[64,512]{0,1:T(8,128)} async-done(((f32[64,512]{0,1:T(8,128)}), f32[64,512]{0,1:T(8,128)}) %all-reduce.13.cloned.1.call-update) | async-done | bytes 131088 | tf_op jit(solution)/shard_map/psum | solution.py:135
  481.4 5.6 convolution_add_fusion.14
  487.0 5.6 convolution_add_fusion.13
  492.6 5.7 fusion.295
  506.7 123.9 %all-reduce.15.cloned.1.call-done = f32[64,512]{0,1:T(8,128)} async-done(((f32[64,512]{0,1:T(8,128)}), f32[64,512]{0,1:T(8,128)}) %all-reduce.15.cloned.1.call-update) | async-done | bytes 131088 | tf_op jit(solution)/shard_map/psum | solution.py:135
  638.0 5.6 convolution_add_fusion.11
  643.6 5.6 convolution_add_fusion.10
  649.2 5.6 fusion.298
  662.2 123.7 %all-reduce.17.cloned.1.call-done = f32[64,512]{0,1:T(8,128)} async-done(((f32[64,512]{0,1:T(8,128)}), f32[64,512]{0,1:T(8,128)}) %all-reduce.17.cloned.1.call-update) | async-done | bytes 131088 | tf_op jit(solution)/shard_map/psum | solution.py:135
  798.9 5.6 convolution_add_fusion.7
  804.4 5.7 fusion.301
  818.5 123.9 %all-reduce.19.cloned.1.call-done = f32[64,512]{0,1:T(8,128)} async-done(((f32[64,512]{0,1:T(8,128)}), f32[64,512]{0,1:T(8,128)}) %all-reduce.19.cloned.1.call-update) | async-done | bytes 131088 | tf_op jit(solution)/shard_map/psum | solution.py:135
  949.9 5.6 convolution_add_fusion.5
  955.5 5.6 convolution_add_fusion.4
  961.0 5.7 fusion.304
  975.2 124.1 %all-reduce.21.cloned.1.call-done = f32[64,512]{0,1:T(8,128)} async-done(((f32[64,512]{0,1:T(8,128)}), f32[64,512]{0,1:T(8,128)}) %all-reduce.21.cloned.1.call-update) | async-done | bytes 131088 | tf_op jit(solution)/shard_map/psum | solution.py:135
  1106.9 5.6 convolution_add_fusion.2
  1112.5 5.6 convolution_add_fusion.1
  1118.1 5.7 fusion.72
  1126.6 52.4 %all_to_all.33 = f32[64,8,1024]{2,1,0:T(8,128)S(1)} all-to-all(f32[64,8,1024]{2,1,0:T(8,128)S(1)} %bitcast.36), channel_id=1, replica_groups=mesh['member'=8,'state'=4] {'member'}, dimensions={0} | all-to-all | bytes 4194304 | tf_op jit(solution)/shard_map/all_to_all | solution.py:151
  (229 shorter events, 240.7 us)
Async XLA Ops:
  9.4 106.3 %collective-permute-start.1 = (f32[8,1,1024]{2,0,1:T(8,128)S(1)}, f32[8,1,1024]{2,0,1:T(8,128)S(1)}, u32[]{:S(2)}, u32[]{:S(2)}) collective-permute-start(f32[8,1,1024]{2,0,1:T(8,128)S(1)} %get-tuple-element.57), channel_id=1, source_target_pairs={{0,1},{1,2},{2,3},{4,5},{5,6},{6,7},{8,9},{9,10},{10,11},{12,13},{... | collective-permute-start | bytes 98312 | tf_op jit(solution)/shard_map/ppermute | solution.py:18
  14.2 101.4 %collective-permute-start = (f32[8,1,1024]{2,0,1:T(8,128)S(1)}, f32[8,1,1024]{2,0,1:T(8,128)S(1)}, u32[]{:S(2)}, u32[]{:S(2)}) collective-permute-start(f32[8,1,1024]{2,0,1:T(8,128)S(1)} %get-tuple-element.56), channel_id=1, source_target_pairs={{1,0},{2,1},{3,2},{5,4},{6,5},{7,6},{9,8},{10,9},{11,10},{13,12},{... | collective-permute-start | bytes 98312 | tf_op jit(solution)/shard_map/ppermute | solution.py:19
  62.8 74.2 %copy-start.15 = (pred[512]{0:T(512)(128)(4,1)}, pred[512]{0:T(512)(128)(4,1)S(1)}, u32[]{:S(2)}) copy-start(pred[512]{0:T(512)(128)(4,1)S(1)} %get-tuple-element.8) | copy-start | bytes 1540
  100.8 14.8 %copy-start.10 = (f32[64,1024]{1,0:T(8,128)S(1)}, f32[64,1024]{1,0:T(8,128)}, u32[]{:S(2)}) copy-start(f32[64,1024]{1,0:T(8,128)} %param.15) | copy-start | bytes 786436
  119.0 7.1 collective-permute-start.3
  123.6 6.2 collective-permute-start.2
  132.1 53.9 %all-to-all-start = ((f32[8,64,1024]{2,0,1:T(8,128)}), f32[8,64,1024]{2,0,1:T(8,128)S(1)}, u32[]{:S(2)}, u32[]{:S(2)}) async-start(f32[8,64,1024]{2,0,1:T(8,128)} %fusion.82), calls=%async_computation | async-start | bytes 4194304 | tf_op jit(solution)/shard_map/all_to_all | solution.py:117
  137.0 180.5 %all-reduce.11.cloned.1.call-start = ((), (), s32[]{:S(2)}) async-start(), calls=%async_computation.2 | async-start | bytes 524288 | tf_op jit(solution)/shard_map/psum | solution.py:135
  192.9 281.1 %all-reduce.13.cloned.1.call-start = ((), (), s32[]{:S(2)}) async-start(), calls=%async_computation.3 | async-start | bytes 524288 | tf_op jit(solution)/shard_map/psum | solution.py:135
  341.7 135.8 %copy-start.6 = (f32[64,8192]{1,0:T(8,128)S(1)}, f32[64,8192]{1,0:T(8,128)}, u32[]{:S(2)}) copy-start(f32[64,8192]{1,0:T(8,128)} %get-tuple-element.201) | copy-start | bytes 6291460
  349.8 280.7 %all-reduce.15.cloned.1.call-start = ((), (), s32[]{:S(2)}) async-start(), calls=%async_computation.4 | async-start | bytes 524288 | tf_op jit(solution)/shard_map/psum | solution.py:135
  498.3 135.8 %copy-start.7 = (f32[64,8192]{1,0:T(8,128)S(1)}, f32[64,8192]{1,0:T(8,128)}, u32[]{:S(2)}) copy-start(f32[64,8192]{1,0:T(8,128)} %get-tuple-element.203) | copy-start | bytes 6291460
  506.4 279.5 %all-reduce.17.cloned.1.call-start = ((), (), s32[]{:S(2)}) async-start(), calls=%async_computation.5 | async-start | bytes 524288 | tf_op jit(solution)/shard_map/psum | solution.py:135
  661.7 280.7 %all-reduce.19.cloned.1.call-start = ((), (), s32[]{:S(2)}) async-start(), calls=%async_computation.6 | async-start | bytes 524288 | tf_op jit(solution)/shard_map/psum | solution.py:135
  810.2 135.8 %copy-start.8 = (f32[64,8192]{1,0:T(8,128)S(1)}, f32[64,8192]{1,0:T(8,128)}, u32[]{:S(2)}) copy-start(f32[64,8192]{1,0:T(8,128)} %get-tuple-element.207) | copy-start | bytes 6291460
  818.3 281.0 %all-reduce.21.cloned.1.call-start = ((), (), s32[]{:S(2)}) async-start(), calls=%async_computation.7 | async-start | bytes 524288 | tf_op jit(solution)/shard_map/psum | solution.py:135
  966.8 134.8 %copy-start.13 = (f32[512]{0:T(512)S(1)}, f32[512]{0:T(512)}, u32[]{:S(2)}) copy-start(f32[512]{0:T(512)} %gather_fusion.34) | copy-start | bytes 6148
  966.8 134.8 %copy-start.14 = (f32[512]{0:T(512)S(1)}, f32[512]{0:T(512)}, u32[]{:S(2)}) copy-start(f32[512]{0:T(512)} %gather_fusion.33) | copy-start | bytes 6148
  966.8 134.8 %copy-start.16 = (pred[512]{0:T(512)(128)(4,1)S(1)}, pred[512]{0:T(512)(128)(4,1)}, u32[]{:S(2)}) copy-start(pred[512]{0:T(512)(128)(4,1)} %copy-done.15) | copy-start | bytes 1540
  966.8 136.1 %copy-start.9 = (f32[64,8192]{1,0:T(8,128)S(1)}, f32[64,8192]{1,0:T(8,128)}, u32[]{:S(2)}) copy-start(f32[64,8192]{1,0:T(8,128)} %get-tuple-element.209) | copy-start | bytes 6291460
  966.8 136.1 %copy-start.25 = (s32[128]{0:T(128)S(1)}, s32[128]{0:T(128)}, u32[]{:S(2)}) copy-start(s32[128]{0:T(128)} %get-tuple-element.101) | copy-start | bytes 1540
  966.8 136.1 %copy-start.26 = (s32[128]{0:T(128)S(1)}, s32[128]{0:T(128)}, u32[]{:S(2)}) copy-start(s32[128]{0:T(128)} %get-tuple-element.237) | copy-start | bytes 1540
  966.8 136.1 %copy-start.30 = (f32[128]{0:T(128)S(1)}, f32[128]{0:T(128)}, u32[]{:S(2)}) copy-start(f32[128]{0:T(128)} %get-tuple-element.109) | copy-start | bytes 1540
  1126.6 53.9 %copy-start.1 = (s32[3072]{0:T(1024)S(1)}, s32[3072]{0:T(1024)}, u32[]{:S(2)}) copy-start(s32[3072]{0:T(1024)} %param.20) | copy-start | bytes 36868
  (18 other events, 125.3 us)
Sparse Core Ops, SparseCore 0:
  193.0 124.3 all-reduce.10
  350.0 123.9 all-reduce.12
  506.5 123.9 all-reduce.14
  661.9 123.9 all-reduce.16
  818.4 123.9 all-reduce.18
  975.3 123.9 all-reduce.20
where the time goes:
time: 1190 us
  waiting for transfers between devices  793 us (67%)
  local copies, waits for them, and re-layouts  149 us (13%)
  matrix products  125 us (11%)
  blocking collectives  52.4 us (4%)
  other arithmetic  34.9 us (3%)
  starting transfers between devices  18.5 us (2%)
  between operations  14.9 us (1%)
    psum x6, waiting for transfers between devices, on_device(): prior_values = lax.psum(local_values, ('member', 'state'))  744 us
    dot_general x24, matrix products, linear_gain_fit(): jnp.dot(increment[:, lower_end:upper_end], gain_tile, preferred_element_t...  125 us
    all_to_all x1, blocking collectives, on_device(): lax.all_to_all(result, 'member', split_axis=0, concat_axis=1, tiled=True)  52.4 us
    all_to_all x1, waiting for transfers between devices, on_device(): lax.all_to_all(realization_vectors, 'member', split_axis=1, concat_axis=0...  45.9 us
  transfers between devices with their start and end apart: 11, of which 8 were waited for; matrix products, arithmetic and copies ran while one was open for 9% of the time, Pallas kernels for 0%

commit v1 on v0

--- a/solution.py
+++ b/solution.py
@@ -6,6 +6,11 @@
 BLK = 512
 NBLK = 6
 spread_eps = 1e-06
+
+
+def by_each_axis(array, inner_axis, outer_axis):
+    half = lax.psum(array, inner_axis)
+    return lax.psum(half, outer_axis)
 
 
 def extended(shard, sides, width):
@@ -132,7 +137,7 @@
         local_values = pick_values(
             cell_values, block_rows, block_cols, first_row, tile_rows, col_count
         )
-        prior_values = lax.psum(local_values, ("member", "state"))
+        prior_values = by_each_axis(local_values, "state", "member")
         anomaly, increment, inverse = increments(
             prior_values, jnp.take(observations, chosen), jnp.take(obs_variance, chosen)
         )

time: 1190 us -> 1010 us (0.85)
  waiting for transfers between devices: 793 us -> 606 us
    psum x6 -> x12, waiting for transfers between devices: 744 us -> 556 us  [the longest x6 342 us: by_each_axis(): return lax.psum(half, outer_axis)]
  transfers between devices with their start and end apart: 11 -> 17, of which waited for: 8 -> 14; matrix products, arithmetic and copies ran while one was open for 9% -> 10% of each run, Pallas kernels for 0% -> 0%
where the time goes in v1:
time: 1010 us; the launch traced here: 996 us
  waiting for transfers between devices  606 us (60%)
  local copies, waits for them, and re-layouts  146 us (14%)
  matrix products  124 us (12%)
  blocking collectives  51.5 us (5%)
  other arithmetic  34.4 us (3%)
  starting transfers between devices  18.9 us (2%)
  between operations  15.1 us (1%)
    psum x6, waiting for transfers between devices, by_each_axis(): return lax.psum(half, outer_axis)  342 us
    psum x6, waiting for transfers between devices, by_each_axis(): half = lax.psum(array, inner_axis)  214 us
    dot_general x24, matrix products, linear_gain_fit(): jnp.dot(increment[:, lower_end:upper_end], gain_tile, preferred_element_t...  124 us
    all_to_all x1, blocking collectives, on_device(): lax.all_to_all(result, 'member', split_axis=0, concat_axis=1, tiled=True)  51.5 us
    all_to_all x1, waiting for transfers between devices, on_device(): lax.all_to_all(realization_vectors, 'member', split_axis=1, concat_axis=0...  46.1 us
  transfers between devices with their start and end apart: 17, of which 14 were waited for; matrix products, arithmetic and copies ran while one was open for 10% of the time, Pallas kernels for 0%

profile of v1, /device:TPU:0, one launch (start us, length us, event | category | flops | bytes accessed | tf_op | source)
XLA Modules:
  0.0 996.3 jit_solution(7791865165341800871)
XLA Ops:
  100.1 46.1 %all-to-all-done = f32[8,64,1024]{2,0,1:T(8,128)S(1)} async-done(((f32[8,64,1024]{2,0,1:T(8,128)}), f32[8,64,1024]{2,0,1:T(8,128)S(1)}, u32[]{:S(2)}, u32[]{:S(2)}) %all-to-all-start) | async-done | bytes 2097184 | tf_op jit(solution)/shard_map/all_to_all | solution.py:122
  159.7 35.9 %all-reduce.17.cloned.1.call-done = f32[64,512]{0,1:T(8,128)} async-done(((f32[64,512]{0,1:T(8,128)}), f32[64,512]{0,1:T(8,128)}) %all-reduce.17.cloned.1.call-update) | async-done | bytes 131088 | tf_op jit(solution)/shard_map/psum | solution.py:12
  195.7 57.2 %all-reduce.19.cloned.1.call-done = f32[64,512]{0,1:T(8,128)} async-done(((f32[64,512]{0,1:T(8,128)}), f32[64,512]{0,1:T(8,128)}) %all-reduce.19.cloned.1.call-update) | async-done | bytes 131088 | tf_op jit(solution)/shard_map/psum | solution.py:13
  271.5 5.7 fusion.292
  291.7 35.7 %all-reduce.21.cloned.1.call-done = f32[64,512]{0,1:T(8,128)} async-done(((f32[64,512]{0,1:T(8,128)}), f32[64,512]{0,1:T(8,128)}) %all-reduce.21.cloned.1.call-update) | async-done | bytes 131088 | tf_op jit(solution)/shard_map/psum | solution.py:12
  327.6 56.9 %all-reduce.23.cloned.1.call-done = f32[64,512]{0,1:T(8,128)} async-done(((f32[64,512]{0,1:T(8,128)}), f32[64,512]{0,1:T(8,128)}) %all-reduce.23.cloned.1.call-update) | async-done | bytes 131088 | tf_op jit(solution)/shard_map/psum | solution.py:13
  403.1 5.7 fusion.295
  423.4 35.7 %all-reduce.25.cloned.1.call-done = f32[64,512]{0,1:T(8,128)} async-done(((f32[64,512]{0,1:T(8,128)}), f32[64,512]{0,1:T(8,128)}) %all-reduce.25.cloned.1.call-update) | async-done | bytes 131088 | tf_op jit(solution)/shard_map/psum | solution.py:12
  459.3 56.9 %all-reduce.27.cloned.1.call-done = f32[64,512]{0,1:T(8,128)} async-done(((f32[64,512]{0,1:T(8,128)}), f32[64,512]{0,1:T(8,128)}) %all-reduce.27.cloned.1.call-update) | async-done | bytes 131088 | tf_op jit(solution)/shard_map/psum | solution.py:13
  523.7 5.6 convolution_add_fusion.11
  529.3 5.6 convolution_add_fusion.10
  534.9 5.6 fusion.298
  553.8 35.7 %all-reduce.29.cloned.1.call-done = f32[64,512]{0,1:T(8,128)} async-done(((f32[64,512]{0,1:T(8,128)}), f32[64,512]{0,1:T(8,128)}) %all-reduce.29.cloned.1.call-update) | async-done | bytes 131088 | tf_op jit(solution)/shard_map/psum | solution.py:12
  590.0 56.8 %all-reduce.31.cloned.1.call-done = f32[64,512]{0,1:T(8,128)} async-done(((f32[64,512]{0,1:T(8,128)}), f32[64,512]{0,1:T(8,128)}) %all-reduce.31.cloned.1.call-update) | async-done | bytes 131088 | tf_op jit(solution)/shard_map/psum | solution.py:13
  654.3 5.6 convolution_add_fusion.8
  659.9 5.6 convolution_add_fusion.7
  665.5 5.6 fusion.301
  690.9 29.2 %all-reduce.33.cloned.1.call-done = f32[64,512]{0,1:T(8,128)} async-done(((f32[64,512]{0,1:T(8,128)}), f32[64,512]{0,1:T(8,128)}) %all-reduce.33.cloned.1.call-update) | async-done | bytes 131088 | tf_op jit(solution)/shard_map/psum | solution.py:12
  720.2 57.1 %all-reduce.35.cloned.1.call-done = f32[64,512]{0,1:T(8,128)} async-done(((f32[64,512]{0,1:T(8,128)}), f32[64,512]{0,1:T(8,128)}) %all-reduce.35.cloned.1.call-update) | async-done | bytes 131088 | tf_op jit(solution)/shard_map/psum | solution.py:13
  795.8 5.7 fusion.304
  810.0 41.8 %all-reduce.37.cloned.1.call-done = f32[64,512]{0,1:T(8,128)} async-done(((f32[64,512]{0,1:T(8,128)}), f32[64,512]{0,1:T(8,128)}) %all-reduce.37.cloned.1.call-update) | async-done | bytes 131088 | tf_op jit(solution)/shard_map/psum | solution.py:12
  851.8 57.1 %all-reduce.39.cloned.1.call-done = f32[64,512]{0,1:T(8,128)} async-done(((f32[64,512]{0,1:T(8,128)}), f32[64,512]{0,1:T(8,128)}) %all-reduce.39.cloned.1.call-update) | async-done | bytes 131088 | tf_op jit(solution)/shard_map/psum | solution.py:13
  927.6 5.7 fusion.72
  936.1 51.5 %all_to_all.33 = f32[64,8,1024]{2,1,0:T(8,128)S(1)} all-to-all(f32[64,8,1024]{2,1,0:T(8,128)S(1)} %bitcast.36), channel_id=1, replica_groups=mesh['member'=8,'state'=4] {'member'}, dimensions={0} | all-to-all | bytes 4194304 | tf_op jit(solution)/shard_map/all_to_all | solution.py:156
  (239 shorter events, 271.2 us)
Async XLA Ops:
  9.4 66.4 %collective-permute-start.1 = (f32[8,1,1024]{2,0,1:T(8,128)S(1)}, f32[8,1,1024]{2,0,1:T(8,128)S(1)}, u32[]{:S(2)}, u32[]{:S(2)}) collective-permute-start(f32[8,1,1024]{2,0,1:T(8,128)S(1)} %get-tuple-element.57), channel_id=1, source_target_pairs={{0,1},{1,2},{2,3},{4,5},{5,6},{6,7},{8,9},{9,10},{10,11},{12,13},{... | collective-permute-start | bytes 98312 | tf_op jit(solution)/shard_map/ppermute | solution.py:23
  14.2 61.6 %collective-permute-start = (f32[8,1,1024]{2,0,1:T(8,128)S(1)}, f32[8,1,1024]{2,0,1:T(8,128)S(1)}, u32[]{:S(2)}, u32[]{:S(2)}) collective-permute-start(f32[8,1,1024]{2,0,1:T(8,128)S(1)} %get-tuple-element.56), channel_id=1, source_target_pairs={{1,0},{2,1},{3,2},{5,4},{6,5},{7,6},{9,8},{10,9},{11,10},{13,12},{... | collective-permute-start | bytes 98312 | tf_op jit(solution)/shard_map/ppermute | solution.py:24
  79.2 6.7 collective-permute-start.3
  83.7 6.2 collective-permute-start.2
  92.3 53.9 %all-to-all-start = ((f32[8,64,1024]{2,0,1:T(8,128)}), f32[8,64,1024]{2,0,1:T(8,128)S(1)}, u32[]{:S(2)}, u32[]{:S(2)}) async-start(f32[8,64,1024]{2,0,1:T(8,128)} %fusion.82), calls=%async_computation | async-start | bytes 4194304 | tf_op jit(solution)/shard_map/all_to_all | solution.py:122
  97.2 98.4 %all-reduce.17.cloned.1.call-start = ((), (), s32[]{:S(2)}) async-start(), calls=%async_computation.2 | async-start | bytes 524288 | tf_op jit(solution)/shard_map/psum | solution.py:12
  153.1 99.8 %all-reduce.19.cloned.1.call-start = ((), (), s32[]{:S(2)}) async-start(), calls=%async_computation.3 | async-start | bytes 524288 | tf_op jit(solution)/shard_map/psum | solution.py:13
  195.6 131.8 %all-reduce.21.cloned.1.call-start = ((), (), s32[]{:S(2)}) async-start(), calls=%async_computation.4 | async-start | bytes 524288 | tf_op jit(solution)/shard_map/psum | solution.py:12
  281.0 107.1 %copy-start.6 = (f32[64,8192]{1,0:T(8,128)S(1)}, f32[64,8192]{1,0:T(8,128)}, u32[]{:S(2)}) copy-start(f32[64,8192]{1,0:T(8,128)} %get-tuple-element.201) | copy-start | bytes 6291460
  285.3 99.3 %all-reduce.23.cloned.1.call-start = ((), (), s32[]{:S(2)}) async-start(), calls=%async_computation.5 | async-start | bytes 524288 | tf_op jit(solution)/shard_map/psum | solution.py:13
  327.4 131.6 %all-reduce.25.cloned.1.call-start = ((), (), s32[]{:S(2)}) async-start(), calls=%async_computation.6 | async-start | bytes 524288 | tf_op jit(solution)/shard_map/psum | solution.py:12
  412.7 107.1 %copy-start.8 = (f32[64,8192]{1,0:T(8,128)S(1)}, f32[64,8192]{1,0:T(8,128)}, u32[]{:S(2)}) copy-start(f32[64,8192]{1,0:T(8,128)} %get-tuple-element.203) | copy-start | bytes 6291460
  417.0 99.2 %all-reduce.27.cloned.1.call-start = ((), (), s32[]{:S(2)}) async-start(), calls=%async_computation.7 | async-start | bytes 524288 | tf_op jit(solution)/shard_map/psum | solution.py:13
  459.1 130.5 %all-reduce.29.cloned.1.call-start = ((), (), s32[]{:S(2)}) async-start(), calls=%async_computation.8 | async-start | bytes 524288 | tf_op jit(solution)/shard_map/psum | solution.py:12
  540.5 119.4 %copy-start.7 = (f32[64,8192]{1,0:T(8,128)}, f32[64,8192]{1,0:T(8,128)S(1)}, u32[]{:S(2)}) copy-start(f32[64,8192]{1,0:T(8,128)S(1)} %get-tuple-element.205) | copy-start | bytes 6291460
  547.4 99.4 %all-reduce.31.cloned.1.call-start = ((), (), s32[]{:S(2)}) async-start(), calls=%async_computation.9 | async-start | bytes 524288 | tf_op jit(solution)/shard_map/psum | solution.py:13
  589.5 130.5 %all-reduce.33.cloned.1.call-start = ((), (), s32[]{:S(2)}) async-start(), calls=%async_computation.10 | async-start | bytes 524288 | tf_op jit(solution)/shard_map/psum | solution.py:12
  678.0 99.2 %all-reduce.35.cloned.1.call-start = ((), (), s32[]{:S(2)}) async-start(), calls=%async_computation.11 | async-start | bytes 524288 | tf_op jit(solution)/shard_map/psum | solution.py:13
  720.1 131.7 %all-reduce.37.cloned.1.call-start = ((), (), s32[]{:S(2)}) async-start(), calls=%async_computation.12 | async-start | bytes 524288 | tf_op jit(solution)/shard_map/psum | solution.py:12
  801.5 109.7 %copy-start.14 = (pred[512]{0:T(512)(128)(4,1)S(1)}, pred[512]{0:T(512)(128)(4,1)}, u32[]{:S(2)}) copy-start(pred[512]{0:T(512)(128)(4,1)} %copy-done.13) | copy-start | bytes 1540
  801.5 111.0 %copy-start.9 = (f32[64,8192]{1,0:T(8,128)S(1)}, f32[64,8192]{1,0:T(8,128)}, u32[]{:S(2)}) copy-start(f32[64,8192]{1,0:T(8,128)} %get-tuple-element.209) | copy-start | bytes 6291460
  801.6 111.0 %copy-start.23 = (s32[128]{0:T(128)S(1)}, s32[128]{0:T(128)}, u32[]{:S(2)}) copy-start(s32[128]{0:T(128)} %get-tuple-element.101) | copy-start | bytes 1540
  801.6 111.0 %copy-start.24 = (s32[128]{0:T(128)S(1)}, s32[128]{0:T(128)}, u32[]{:S(2)}) copy-start(s32[128]{0:T(128)} %get-tuple-element.237) | copy-start | bytes 1540
  809.7 99.3 %all-reduce.39.cloned.1.call-start = ((), (), s32[]{:S(2)}) async-start(), calls=%async_computation.13 | async-start | bytes 524288 | tf_op jit(solution)/shard_map/psum | solution.py:13
  (20 other events, 290.7 us)
Sparse Core Ops, SparseCore 0:
  153.2 42.3 all-reduce.16
  198.0 54.8 all-reduce.18
  285.4 41.9 all-reduce.20
  329.7 54.8 all-reduce.22
  417.1 41.8 all-reduce.24
  461.3 54.8 all-reduce.26
  547.6 41.9 all-reduce.28
  591.9 54.8 all-reduce.30
  678.1 41.9 all-reduce.32
  722.4 54.8 all-reduce.34
  809.8 41.9 all-reduce.36
  854.1 54.8 all-reduce.38
